TPU v7x, 1024 devices: a whole 8x8x8 slice. The times are simulated.
1024 devices in a mesh: dp: 64 (over y, z), mp: 16 (over x, core).
Axes of the slice: x: 8, y: 8, z: 8, core: 2. Of those that a mesh axis runs over, the one named last changes fastest.
Arguments:
- cotangent: bfloat16 [16384, 5376], P('dp', 'mp')
- token_ids: int32 [16384], P('dp'), may hold values from 0 to 32767, as said below
- block_counts: int32 [64, 128], P('dp'), may hold values from 0 to 8, as said below
- block_slot: int32 [128], replicated, may hold values from 0 to 127, as said below
- table: bfloat16 [32768, 5376], P('dp', 'mp'), may hold values from -6 to 6
- m_code: bfloat16 [32768, 5376], P('dp', 'mp'), may hold values from -1 to 1
- m_scale: float32 [32768], P('dp'), may hold values from 0.05 to 0.5
- v_code: bfloat16 [32768, 5376], P('dp', 'mp'), may hold values from 0.25 to 1
- v_scale: float32 [32768], P('dp'), may hold values from 0.3 to 3
Outputs:
- new_table: bfloat16 [32768, 5376], P('dp', 'mp')
- new_m_code: bfloat16 [32768, 5376], P('dp', 'mp')
- new_m_scale: float32 [32768], P('dp')
- new_v_code: bfloat16 [32768, 5376], P('dp', 'mp')
- new_v_scale: float32 [32768], P('dp')
Inputs may be any that keep to these rules, and one draw needn't show every extreme that they name: `token_ids`: within each shard of 256 tokens the ids are sorted ascending. block_counts[d, b] is the number of ids of shard d in vocabulary block b (ids b * 256 to b * 256 + 255), so each row sums to 256. The table rows of vocabulary block b lie on index block_slot[b] // 2 of dp; the tokens of one shard whose rows lie on one index of dp number at most 8. `block_slot`: A permutation of 0 to 127.
All inputs are finite; a program needn't handle non-finite values. Where the computation divides by a largest or mean magnitude, that divisor is 1e-20 or more.
Results may differ from a plain program's by a relative error of at most 0.0025.
Values may be sent and summed in bfloat16 or wider, within the bound.
A program may use at most 32 MiB of HBM per device.

v0:
```python
import jax
import jax.numpy as jnp
from jax import lax
from jax.sharding import PartitionSpec as P

BLOCK = 256


beta_first = 0.9
beta_second = 0.95
step_rate = 0.05
eps_root = 1e-08
eps_peak = 1e-06


def moments(gradient, table_cols, mcode_cols, mscale, vcode_cols, vscale):
    moment = beta_first * (mcode_cols.astype(jnp.float32) * mscale[:, None]) + 0.1 * gradient
    second = beta_second * (vcode_cols.astype(jnp.float32) * vscale[:, None]) + 0.05 * (
        gradient * gradient
    )
    updated = (
        table_cols.astype(jnp.float32) - step_rate * (moment / (jnp.sqrt(second) + eps_root))
    ).astype(jnp.bfloat16)
    return (updated, moment, second)


def per_device(
    cotangent, token_ids, block_counts, block_slot, table, m_code, m_scale, v_code, v_scale
):
    n_owners = lax.axis_size("dp")
    tok_count = token_ids.shape[0]
    rows_own = table.shape[0]
    blk_own = rows_own // BLOCK
    capacity = 2 * (tok_count // n_owners)
    counts = block_counts[0]
    n_blocks = counts.shape[0]
    starts = jnp.cumsum(counts) - counts
    block_ids = jnp.arange(n_blocks, dtype=jnp.int32)
    stored = block_slot[None, :] == block_ids[:, None]
    own_counts = jnp.sum(jnp.where(stored, counts[None, :], 0), axis=1).reshape(n_owners, blk_own)
    own_starts = jnp.sum(jnp.where(stored, starts[None, :], 0), axis=1).reshape(n_owners, blk_own)
    before = jnp.cumsum(own_counts, axis=1) - own_counts
    totals = jnp.sum(own_counts, axis=1)
    slot_ids = jnp.arange(capacity, dtype=jnp.int32)
    sub_block = jnp.sum((slot_ids[None, :, None] >= before[:, None, 1:]).astype(jnp.int32), axis=2)
    filled = slot_ids[None, :] < totals[:, None]
    first_tok = jnp.take_along_axis(own_starts, sub_block, axis=1)
    offset_in = slot_ids[None, :] - jnp.take_along_axis(before, sub_block, axis=1)
    source = jnp.where(filled, first_tok + offset_in, 0)
    sent_rows = cotangent[source]
    sent_index = jnp.where(filled, sub_block * BLOCK + token_ids[source] % BLOCK, rows_own)
    recv_rows, recv_index = (
        lax.all_to_all(sent_rows, "dp", split_axis=0, concat_axis=0, tiled=True),
        lax.all_to_all(sent_index, "dp", split_axis=0, concat_axis=0, tiled=True),
    )
    flat_rows = recv_rows.reshape(-1, recv_rows.shape[-1])
    flat_index = recv_index.reshape(-1)
    targets = jnp.arange(rows_own, dtype=jnp.int32)
    selector = (targets[:, None] == flat_index[None, :]).astype(jnp.bfloat16)
    gradient = jnp.dot(selector, flat_rows, preferred_element_type=jnp.float32)
    new_table, moment, second = moments(gradient, table, m_code, m_scale, v_code, v_scale)
    local_m_peak = jnp.max(jnp.abs(moment), axis=1)
    local_v_peak = jnp.max(second, axis=1)
    new_m_scale, new_v_scale = lax.pmax((local_m_peak, local_v_peak), "mp")
    new_m_code = (moment / (new_m_scale[:, None] + eps_peak)).astype(jnp.bfloat16)
    new_v_code = (second / (new_v_scale[:, None] + eps_peak)).astype(jnp.bfloat16)
    return (new_table, new_m_code, new_m_scale, new_v_code, new_v_scale)


def solution(mesh):
    return jax.shard_map(
        per_device,
        mesh=mesh,
        in_specs=(
            P("dp", "mp"),
            P("dp"),
            P("dp", None),
            P(),
            P("dp", "mp"),
            P("dp", "mp"),
            P("dp"),
            P("dp", "mp"),
            P("dp"),
        ),
        out_specs=(P("dp", "mp"), P("dp", "mp"), P("dp"), P("dp", "mp"), P("dp")),
        check_vma=False,
    )
```

profile of v0, /device:TPU:1, one launch (start us, length us, event | category | flops | bytes accessed | tf_op | source)
XLA Modules:
  0.0 99.7 jit_solution(17135183698053863845)
XLA Ops:
  0.7 1.0 %reduce-window_clone.1 = s32[1,128]{1,0:T(1,128)S(1)} reduce-window(s32[1,128]{1,0:T(1,128)} %param.13, s32[]{:T(128)} %constant.20.clone.1), window={size=1x128 pad=0_0x127_0}, to_apply=%region_3.4 | reduce-window | flops 16256 | bytes 1028 | tf_op jit(solution)/shard_map/reduce-window.clone
  1.7 0.7 copy-done.9
  2.3 0.1 select_reduce_fusion
  2.4 0.1 reshape.170
  2.6 0.1 reshape.169
  2.7 0.2 reduce_window_sum.18
  2.9 0.1 fusion.12
  3.0 0.2 slice_reduce_fusion
  3.4 3.8 %gather_fusion.3 = s32[512]{0:T(512)S(1)} fusion(s32[64,2]{1,0:T(8,128)S(1)} %get-tuple-element.16, s32[512]{0:T(512)S(1)} %reshape.217), kind=kCustom, calls=%fused_computation.1.clone | custom fusion | bytes 8192 | tf_op jit(solution)/shard_map/jit(take_along_axis)/gather | solution.py:48
  7.2 3.8 %gather_fusion.2 = s32[512]{0:T(512)S(1)} fusion(s32[64,2]{1,0:T(8,128)S(1)} %reshape.170, s32[512]{0:T(512)S(1)} %reshape.217), kind=kCustom, calls=%fused_computation.clone | custom fusion | bytes 8192 | tf_op jit(solution)/shard_map/jit(take_along_axis)/gather | solution.py:47
  11.3 3.5 %gather_fusion = s32[512]{0:T(512)S(1)} fusion(s32[256]{0:T(256)S(1)} %copy-done, s32[1024]{0:T(1024)S(1)} %pad_clamp_fusion), kind=kCustom, calls=%fused_computation.2 | custom fusion | bytes 6144 | tf_op jit(solution)/shard_map/gather | solution.py:51
  14.9 0.7 fusion.5
  15.6 24.0 %all-to-all-start = ((s32[64,1,8]{2,1,0:T(1,128)}), s32[64,1,8]{2,1,0:T(1,128)S(1)}, u32[]{:S(2)}, u32[]{:S(2)}) async-start(s32[64,1,8]{2,1,0:T(1,128)} %bitcast.4), calls=%async_computation | async-start | bytes 65536 | tf_op jit(solution)/shard_map/all_to_all | solution.py:54
  39.6 0.2 copy.19
  39.8 2.6 %gather_fusion.1 = bf16[512,336]{1,0:T(8,128)(2,1)} fusion(bf16[256,336]{1,0:T(8,128)(2,1)S(1)} %copy.19, s32[1024]{0:T(1024)S(1)} %pad_clamp_fusion), kind=kCustom, calls=%fused_computation.3 | custom fusion | bytes 690176 | tf_op jit(solution)/shard_map/gather | solution.py:50
  42.4 8.0 %all-to-all-done = s32[64,1,8]{2,1,0:T(1,128)S(1)} async-done(((s32[64,1,8]{2,1,0:T(1,128)}), s32[64,1,8]{2,1,0:T(1,128)S(1)}, u32[]{:S(2)}, u32[]{:S(2)}) %all-to-all-start) | async-done | bytes 2080 | tf_op jit(solution)/shard_map/all_to_all | solution.py:54
  50.4 4.8 %all-to-all-start.1 = ((bf16[64,8,336]{2,1,0:T(8,128)(2,1)}), bf16[64,8,336]{2,1,0:T(8,128)(2,1)S(1)}, u32[]{:S(2)}, u32[]{:S(2)}) async-start(bf16[64,8,336]{2,1,0:T(8,128)(2,1)} %bitcast.5), calls=%async_computation.1 | async-start | bytes 786432 | tf_op jit(solution)/shard_map/all_to_all | solution.py:53
  55.2 0.5 broadcast.215
  55.7 0.7 reduce.5
  56.5 12.3 %all-to-all-done.1 = bf16[64,8,336]{2,1,0:T(8,128)(2,1)S(1)} async-done(((bf16[64,8,336]{2,1,0:T(8,128)(2,1)}), bf16[64,8,336]{2,1,0:T(8,128)(2,1)S(1)}, u32[]{:S(2)}, u32[]{:S(2)}) %all-to-all-start.1) | async-done | bytes 344096 | tf_op jit(solution)/shard_map/all_to_all | solution.py:53
  68.8 1.7 %fusion.11 = (f32[512]{0:T(512)S(1)}, f32[512]{0:T(512)S(1)}, bf16[512,336]{0,1:T(8,128)(2,1)}, f32[512,336]{0,1:T(8,128)S(1)}) fusion(f32[512]{0:T(512)S(1)} %copy-done.6, bf16[512,336]{0,1:T(8,128)(2,1)S(1)} %copy-done.1, f32[512]{0:T(512)S(1)} %copy-done.7, bf16[512,336]{0,1:T(8,128)(2,1)S(1)} %copy-done.2, bf16[512,336]{0,1:T(8,128)(2,1)S(1)} %copy-done.10, ...), kind=kOutput, calls=%fused_computation.41 | convolution fusion | flops 179862528 | bytes 2418688 | tf_op jit(solution)/shard_map/dot_general | solution.py:60
  70.5 27.5 %all-reduce = (f32[512]{0:T(512)S(1)}, f32[512]{0:T(512)S(1)}) all-reduce(f32[512]{0:T(512)S(1)} %get-tuple-element.7, f32[512]{0:T(512)S(1)} %get-tuple-element.6), channel_id=1, replica_groups=mesh['dp'=64,'mp'=16] {'mp'}, use_global_device_ids=true, to_apply=%region_6.8 | all-reduce | flops 1024 | bytes 8192 | tf_op jit(solution)/shard_map/pmax | solution.py:64
  98.0 0.6 copy-done.4
  98.5 1.2 %divide_convert_fusion = (bf16[512,336]{0,1:T(8,128)(2,1)}, bf16[512,336]{0,1:T(8,128)(2,1)}) fusion(f32[512]{0:T(512)S(1)} %get-tuple-element.18, f32[512,336]{0,1:T(8,128)S(1)} %get-tuple-element.17, f32[512]{0:T(512)S(1)} %copy-done.6, bf16[512,336]{0,1:T(8,128)(2,1)S(1)} %copy-done.1, f32[512]{0:T(512)S(1)} %get-tuple-element.19, f32[512]{0:T(512)S(1)} %copy-done.7, ...), kind=kLoop, calls=%fused_computation.6 | loop fusion | flops 2580480 | bytes 2072576 | tf_op jit(solution)/shard_map/convert_element_type | solution.py:66
  (31 shorter events, 0.8 us)
Async XLA Ops:
  0.6 10.7 %copy-start = (s32[256]{0:T(256)S(1)}, s32[256]{0:T(256)}, u32[]{:S(2)}) copy-start(s32[256]{0:T(256)} %param.12) | copy-start | bytes 3076
  0.6 1.0 %copy-start.8 = (s32[1,128]{1,0:T(1,128)S(1)}, s32[1,128]{1,0:T(1,128)}, u32[]{:S(2)}) copy-start(s32[1,128]{1,0:T(1,128)} %param.13) | copy-start | bytes 1540
  1.7 0.7 copy-start.9
  11.3 28.3 %copy-start.3 = (bf16[256,336]{0,1:T(8,128)(2,1)S(1)}, bf16[256,336]{0,1:T(8,128)(2,1)}, u32[]{:S(2)}) copy-start(bf16[256,336]{0,1:T(8,128)(2,1)} %param.11) | copy-start | bytes 516100
  15.6 34.7 %all-to-all-start = ((s32[64,1,8]{2,1,0:T(1,128)}), s32[64,1,8]{2,1,0:T(1,128)S(1)}, u32[]{:S(2)}, u32[]{:S(2)}) async-start(s32[64,1,8]{2,1,0:T(1,128)} %bitcast.4), calls=%async_computation | async-start | bytes 65536 | tf_op jit(solution)/shard_map/all_to_all | solution.py:54
  39.8 29.0 %copy-start.10 = (bf16[512,336]{0,1:T(8,128)(2,1)S(1)}, bf16[512,336]{0,1:T(8,128)(2,1)}, u32[]{:S(2)}) copy-start(bf16[512,336]{0,1:T(8,128)(2,1)} %param.15) | copy-start | bytes 1032196
  50.4 18.4 %copy-start.1 = (bf16[512,336]{0,1:T(8,128)(2,1)S(1)}, bf16[512,336]{0,1:T(8,128)(2,1)}, u32[]{:S(2)}) copy-start(bf16[512,336]{0,1:T(8,128)(2,1)} %param.18) | copy-start | bytes 1032196
  50.4 18.4 %copy-start.2 = (bf16[512,336]{0,1:T(8,128)(2,1)S(1)}, bf16[512,336]{0,1:T(8,128)(2,1)}, u32[]{:S(2)}) copy-start(bf16[512,336]{0,1:T(8,128)(2,1)} %param.16) | copy-start | bytes 1032196
  50.4 18.4 %all-to-all-start.1 = ((bf16[64,8,336]{2,1,0:T(8,128)(2,1)}), bf16[64,8,336]{2,1,0:T(8,128)(2,1)S(1)}, u32[]{:S(2)}, u32[]{:S(2)}) async-start(bf16[64,8,336]{2,1,0:T(8,128)(2,1)} %bitcast.5), calls=%async_computation.1 | async-start | bytes 786432 | tf_op jit(solution)/shard_map/all_to_all | solution.py:53
  56.4 12.4 %copy-start.6 = (f32[512]{0:T(512)S(1)}, f32[512]{0:T(512)}, u32[]{:S(2)}) copy-start(f32[512]{0:T(512)} %param.19) | copy-start | bytes 6148
  56.4 12.4 %copy-start.7 = (f32[512]{0:T(512)S(1)}, f32[512]{0:T(512)}, u32[]{:S(2)}) copy-start(f32[512]{0:T(512)} %param.17) | copy-start | bytes 6148
  97.9 0.6 copy-start.4
  97.9 0.6 copy-start.5
where the time goes:
time: 100 us; the launch traced here: 99.7 us
  starting transfers between devices  28.7 us (29%)
  blocking collectives  27.5 us (28%)
  waiting for transfers between devices  20.3 us (20%)
  local copies, waits for them, and re-layouts  16.5 us (16%)
  other arithmetic  4.2 us (4%)
  matrix products  1.65 us (2%)
    pmax x1, blocking collectives, per_device(): new_m_scale, new_v_scale = lax.pmax((local_m_peak, local_v_peak), 'mp')  27.5 us
    all_to_all x1, starting transfers between devices, per_device(): lax.all_to_all(sent_index, 'dp', split_axis=0, concat_axis=0, tiled=True)  24 us
    all_to_all x1, waiting for transfers between devices, per_device(): lax.all_to_all(sent_rows, 'dp', split_axis=0, concat_axis=0, tiled=True)  12.3 us
    all_to_all x1, waiting for transfers between devices, per_device(): lax.all_to_all(sent_index, 'dp', split_axis=0, concat_axis=0, tiled=True)  8 us
    all_to_all x1, starting transfers between devices, per_device(): lax.all_to_all(sent_rows, 'dp', split_axis=0, concat_axis=0, tiled=True)  4.76 us
    gather x3, local copies, waits for them, and re-layouts, per_device(): first_tok = jnp.take_along_axis(own_starts, sub_block, axis=1)  3.94 us
    gather x2, local copies, waits for them, and re-layouts, per_device(): jnp.take_along_axis(before, sub_block, axis=1)  3.85 us
    gather x2, local copies, waits for them, and re-layouts, per_device(): token_ids[source] % BLOCK  3.59 us
  transfers between devices with their start and end apart: 2, of which 2 were waited for; matrix products, arithmetic and copies ran while one was open for 4% of the time, Pallas kernels for 0%

commit v1 on v0

v1 whole, which is shorter than its diff:
```python
import functools

import jax
import jax.numpy as jnp
from jax import lax
from jax.experimental import pallas as pl
from jax.experimental.pallas import tpu as pltpu
from jax.sharding import PartitionSpec as P

BLOCK = 256
CAP = 8
LANES = 128
MESH = pl.DeviceIdType.MESH

beta_first = 0.9
beta_second = 0.95
step_rate = 0.05
eps_root = 1e-08
eps_peak = 1e-06


def kernel(
    n_dp, n_mp,
    cot_hbm, tok_hbm, slot_hbm, tab_hbm, mc_hbm, ms_hbm, vc_hbm, vs_hbm,
    nt_hbm, nm_hbm, nms_hbm, nv_hbm, nvs_hbm,
    cot, tok, slot, tab, mc, ms, vc, vs,
    send, recv, mom, sec, peak, peaks, nt, nm, nv, nms, nvs,
    in_sems, out_sems, send_sem, recv_sem, psend_sem, precv_sem,
):
    dp, mp = lax.axis_index("dp"), lax.axis_index("mp")
    width, n_tok = cot.shape
    rows = tab.shape[1]
    n_blk = slot.shape[1]
    n_slot = n_dp * CAP
    full = send.shape[2]
    n_meta = full - width
    strip = 48 if width % 48 == 0 else 16

    barrier = pltpu.get_barrier_semaphore()

    def greet_dp(i, _):
        pl.semaphore_signal(barrier, inc=1, device_id={"dp": lax.rem(dp + i, n_dp)}, device_id_type=MESH)
        return 0

    def greet_mp(i, _):
        pl.semaphore_signal(barrier, inc=1, device_id={"mp": lax.rem(mp + i, n_mp)}, device_id_type=MESH)
        return 0

    copies = [
        pltpu.make_async_copy(src, dst, in_sems.at[i])
        for i, (src, dst) in enumerate(
            ((tok_hbm, tok), (slot_hbm, slot), (cot_hbm, cot), (ms_hbm, ms), (vs_hbm, vs), (mc_hbm, mc), (vc_hbm, vc), (tab_hbm, tab))
        )
    ]
    for copy in copies:
        copy.start()
    lax.fori_loop(1, n_dp, greet_dp, 0)
    lax.fori_loop(1, n_mp, greet_mp, 0)

    copies[0].wait()
    copies[1].wait()
    ids = tok[...]
    low = ids % BLOCK
    blk = ids // BLOCK
    in_block = (lax.broadcasted_iota(jnp.int32, (n_blk, n_tok), 0) == blk).astype(jnp.bfloat16)
    slot_rows = jnp.broadcast_to(slot[...].astype(jnp.float32), (16, n_blk)).astype(jnp.bfloat16)
    held = jnp.dot(slot_rows, in_block, preferred_element_type=jnp.float32)[0:1, :].astype(jnp.int32)
    owner = held // 2
    sub = held % 2
    of_owner = (lax.broadcasted_iota(jnp.int32, (n_dp, n_tok), 0) == owner).astype(jnp.float32)
    earlier = (
        lax.broadcasted_iota(jnp.int32, (n_tok, n_tok), 0) < lax.broadcasted_iota(jnp.int32, (n_tok, n_tok), 1)
    ).astype(jnp.bfloat16)
    before = jnp.dot(of_owner.astype(jnp.bfloat16), earlier, preferred_element_type=jnp.float32)
    rank = jnp.sum(of_owner * before, axis=0, keepdims=True)
    place = owner * CAP + rank.astype(jnp.int32)
    chosen = (lax.broadcasted_iota(jnp.int32, (n_slot, n_tok), 0) == place).astype(jnp.bfloat16)

    meta_row = lax.broadcasted_iota(jnp.int32, (n_meta, n_tok), 0)
    meta = jnp.where(meta_row == 0, low, jnp.where(meta_row == 1, (sub + 1) * BLOCK, 0))
    meta = meta.astype(jnp.float32).astype(jnp.bfloat16)
    copies[2].wait()
    tokens = jnp.concatenate([cot[...], meta], axis=0)
    sent = lax.dot_general(chosen, tokens, (((1,), (1,)), ((), ())), preferred_element_type=jnp.float32)
    send[...] = sent.reshape(n_dp, CAP, full).astype(jnp.bfloat16)

    pl.semaphore_wait(barrier, n_dp + n_mp - 2)

    def send_rows(i, _):
        to = lax.rem(dp + i, n_dp)
        pltpu.make_async_remote_copy(
            src_ref=send.at[to], dst_ref=recv.at[dp], send_sem=send_sem, recv_sem=recv_sem,
            device_id={"dp": to}, device_id_type=MESH,
        ).start()
        return 0

    lax.fori_loop(1, n_dp, send_rows, 0)
    recv[pl.ds(dp, 1)] = send[pl.ds(dp, 1)]

    for copy in copies[3:]:
        copy.wait()
    for c in range(0, width, strip):
        at = pl.ds(c, strip)
        mom[at, :] = beta_first * (mc[at, :].astype(jnp.float32) * ms[...])
        sec[at, :] = beta_second * (vc[at, :].astype(jnp.float32) * vs[...])

    others = pl.ds(0, n_dp - 1)
    pltpu.make_async_copy(recv.at[others], recv.at[others], recv_sem).wait()

    got = recv[...].astype(jnp.float32).reshape(n_slot, full).astype(jnp.bfloat16)
    last = full - LANES
    pick = (lax.broadcasted_iota(jnp.int32, (LANES, rows), 0) >= width - last).astype(jnp.bfloat16)
    index = jnp.dot(got[:, last:full], pick, preferred_element_type=jnp.float32).astype(jnp.int32)
    row = lax.broadcasted_iota(jnp.int32, (n_slot, rows), 1) + BLOCK
    selector = (row == index).astype(jnp.bfloat16)
    grad = lax.dot_general(got, selector, (((0,), (0,)), ((), ())), preferred_element_type=jnp.float32)

    m_top = jnp.zeros((8, rows), jnp.float32)
    v_top = jnp.zeros((8, rows), jnp.float32)
    for c in range(0, width, strip):
        at = pl.ds(c, strip)
        g = grad[c : c + strip]
        moment = mom[at, :] + 0.1 * g
        second = sec[at, :] + 0.05 * (g * g)
        mom[at, :] = moment
        sec[at, :] = second
        m_top = jnp.maximum(m_top, jnp.max(jnp.abs(moment).reshape(strip // 8, 8, rows), axis=0))
        v_top = jnp.maximum(v_top, jnp.max(second.reshape(strip // 8, 8, rows), axis=0))
    peak[0:1, :] = jnp.max(m_top, axis=0, keepdims=True)
    peak[1:2, :] = jnp.max(v_top, axis=0, keepdims=True)

    def send_peak(i, _):
        to = lax.rem(mp + i, n_mp)
        pltpu.make_async_remote_copy(
            src_ref=peak, dst_ref=peaks.at[mp], send_sem=psend_sem, recv_sem=precv_sem,
            device_id={"mp": to}, device_id_type=MESH,
        ).start()
        return 0

    lax.fori_loop(1, n_mp, send_peak, 0)
    peaks[pl.ds(mp, 1)] = peak[...][None]

    for c in range(0, width, strip):
        at = pl.ds(c, strip)
        moment, second = mom[at, :], sec[at, :]
        nt[at, :] = (tab[at, :].astype(jnp.float32) - step_rate * (moment / (jnp.sqrt(second) + eps_root))).astype(jnp.bfloat16)
    outs = [
        pltpu.make_async_copy(src, dst, out_sems.at[i])
        for i, (src, dst) in enumerate(((nt, nt_hbm), (nms, nms_hbm), (nvs, nvs_hbm), (nm, nm_hbm), (nv, nv_hbm)))
    ]
    outs[0].start()

    others = pl.ds(0, n_mp - 1)
    pltpu.make_async_copy(peaks.at[others], peaks.at[others], precv_sem).wait()
    top = jnp.max(peaks[...], axis=0)
    m_peak, v_peak = top[0:1], top[1:2]
    nms[...] = m_peak
    nvs[...] = v_peak
    outs[1].start()
    outs[2].start()
    m_peak, v_peak = m_peak + eps_peak, v_peak + eps_peak
    for c in range(0, width, strip):
        at = pl.ds(c, strip)
        nm[at, :] = (mom[at, :] / m_peak).astype(jnp.bfloat16)
        nv[at, :] = (sec[at, :] / v_peak).astype(jnp.bfloat16)
    outs[3].start()
    outs[4].start()
    pltpu.make_async_copy(peaks.at[others], peaks.at[others], psend_sem).wait()
    others = pl.ds(0, n_dp - 1)
    pltpu.make_async_copy(send.at[others], send.at[others], send_sem).wait()
    for out in outs:
        out.wait()


def per_device(cotangent, token_ids, block_counts, block_slot, table, m_code, m_scale, v_code, v_scale):
    del block_counts
    n_dp, n_mp = lax.axis_size("dp"), lax.axis_size("mp")
    n_tok, width = cotangent.shape
    rows = table.shape[0]
    full = width // LANES * LANES + LANES
    bf, f32, i32 = jnp.bfloat16, jnp.float32, jnp.int32
    wide, line = (width, rows), (1, rows)
    outs = pl.pallas_call(
        functools.partial(kernel, n_dp, n_mp),
        out_shape=(
            jax.ShapeDtypeStruct(wide, bf),
            jax.ShapeDtypeStruct(wide, bf),
            jax.ShapeDtypeStruct(line, f32),
            jax.ShapeDtypeStruct(wide, bf),
            jax.ShapeDtypeStruct(line, f32),
        ),
        in_specs=[pl.BlockSpec(memory_space=pltpu.HBM)] * 8,
        out_specs=[pl.BlockSpec(memory_space=pltpu.HBM)] * 5,
        scratch_shapes=[
            pltpu.VMEM((width, n_tok), bf),
            pltpu.VMEM((1, n_tok), i32),
            pltpu.VMEM((1, block_slot.shape[0]), i32),
            pltpu.VMEM(wide, bf),
            pltpu.VMEM(wide, bf),
            pltpu.VMEM(line, f32),
            pltpu.VMEM(wide, bf),
            pltpu.VMEM(line, f32),
            pltpu.VMEM((n_dp, CAP, full), bf),
            pltpu.VMEM((n_dp, CAP, full), bf),
            pltpu.VMEM(wide, f32),
            pltpu.VMEM(wide, f32),
            pltpu.VMEM((2, rows), f32),
            pltpu.VMEM((n_mp, 2, rows), f32),
            pltpu.VMEM(wide, bf),
            pltpu.VMEM(wide, bf),
            pltpu.VMEM(wide, bf),
            pltpu.VMEM(line, f32),
            pltpu.VMEM(line, f32),
            pltpu.SemaphoreType.DMA((8,)),
            pltpu.SemaphoreType.DMA((5,)),
            pltpu.SemaphoreType.DMA,
            pltpu.SemaphoreType.DMA,
            pltpu.SemaphoreType.DMA,
            pltpu.SemaphoreType.DMA,
        ],
        compiler_params=pltpu.CompilerParams(
            collective_id=0, has_side_effects=True, vmem_limit_bytes=63 * 1024 * 1024
        ),
        name="embed_adam",
    )(
        cotangent.T, token_ids.reshape(1, -1), block_slot.reshape(1, -1), table.T,
        m_code.T, m_scale.reshape(line), v_code.T, v_scale.reshape(line),
    )
    new_table, new_m_code, new_m_scale, new_v_code, new_v_scale = outs
    return (new_table.T, new_m_code.T, new_m_scale.reshape(rows), new_v_code.T, new_v_scale.reshape(rows))


def solution(mesh):
    return jax.shard_map(
        per_device,
        mesh=mesh,
        in_specs=(
            P("dp", "mp"),
            P("dp"),
            P("dp", None),
            P(),
            P("dp", "mp"),
            P("dp", "mp"),
            P("dp"),
            P("dp", "mp"),
            P("dp"),
        ),
        out_specs=(P("dp", "mp"), P("dp", "mp"), P("dp"), P("dp", "mp"), P("dp")),
        check_vma=False,
    )
```

time: 100 us -> 50.3 us (0.50)
  Pallas kernels: 0 us -> 45.1 us
  starting transfers between devices: 28.7 us -> 0 us
  blocking collectives: 27.5 us -> 0 us
  waiting for transfers between devices: 20.3 us -> 0 us
  local copies, waits for them, and re-layouts: 16.5 us -> 4.41 us
  other arithmetic: 4.2 us -> 0 us
  matrix products: 1.65 us -> 0 us
    pallas_call x0 -> x1, Pallas kernels: none -> 45.1 us  [per_device(): pl.pallas_call(functools.partial(kernel, n_dp, n_mp), out_shape=(jax.Shap...]
    all_to_all x2 -> x0, starting transfers between devices: 28.7 us -> none  [the longest x1 24 us: per_device(): lax.all_to_all(sent_index, 'dp', split_axis=0, concat_axis=0, tiled=True)]
    pmax x1 -> x0, blocking collectives: 27.5 us -> none  [per_device(): new_m_scale, new_v_scale = lax.pmax((local_m_peak, local_v_peak), 'mp')]
    all_to_all x2 -> x0, waiting for transfers between devices: 20.3 us -> none  [the longest x1 12.3 us: per_device(): lax.all_to_all(sent_rows, 'dp', split_axis=0, concat_axis=0, tiled=True)]
    gather x8 -> x0, local copies, waits for them, and re-layouts: 14 us -> none  [the longest x3 3.94 us: per_device(): first_tok = jnp.take_along_axis(own_starts, sub_block, axis=1)]
    unnamed x23 -> x13, local copies, waits for them, and re-layouts: 1.43 us -> 4.41 us
    dot_general x1 -> x0, matrix products: 1.65 us -> none  [per_device(): gradient = jnp.dot(selector, flat_rows, preferred_element_type=jnp.float32)]
    another operation x2 -> x0, other arithmetic: 1.18 us -> none
  transfers between devices with their start and end apart: 2 -> 0, of which waited for: 2 -> 0; matrix products, arithmetic and copies ran while one was open for 4% -> 0% of each run, Pallas kernels for 0% -> 0%
where the time goes in v1:
time: 50.3 us; the launch traced here: 50.2 us
  Pallas kernels  45.1 us (90%)
  local copies, waits for them, and re-layouts  4.41 us (9%)
  between operations  0.66 us (1%)
    pallas_call x1, Pallas kernels, per_device(): pl.pallas_call(functools.partial(kernel, n_dp, n_mp), out_shape=(jax.Shap...  45.1 us
    unnamed x13, local copies, waits for them, and re-layouts  4.41 us

profile of v1, /device:TPU:1, one launch (start us, length us, event | category | flops | bytes accessed | tf_op | source)
XLA Modules:
  0.0 50.2 jit_solution(11928931239215350072)
XLA Ops:
  0.6 45.1 %embed_adam.1 = (bf16[336,512]{1,0:T(8,128)(2,1)}, bf16[336,512]{1,0:T(8,128)(2,1)}, f32[1,512]{1,0:T(1,128)}, bf16[336,512]{1,0:T(8,128)(2,1)}, f32[1,512]{1,0:T(1,128)}) custom-call(bf16[336,256]{1,0:T(8,128)(2,1)} %bitcast.19, s32[1,256]{1,0:T(1,128)} %bitcast.24, s32[1,128]{1,0:T(1,128)} %bitcast.25, bf16[336,512]{1,0:T(8,128)(2,1)} %bitcast.13, ...), custom_call_target="tpu_custom_call" | custom-call | tf_op jit(solution)/shard_map/embed_adam/pallas_call | solution.py:183
  45.7 0.0 copy-start.1
  45.7 1.8 %copy.18 = bf16[512,336]{0,1:T(8,128)(2,1)} copy(bf16[512,336]{0,1:T(8,128)(2,1)} %bitcast.18) | data formatting | bytes 688128
  47.5 0.0 copy-done.1
  47.5 0.0 copy-start.3
  47.5 0.0 copy-start
  47.5 0.7 %copy.19 = bf16[512,336]{0,1:T(8,128)(2,1)} copy(bf16[512,336]{0,1:T(8,128)(2,1)S(1)} %bitcast.17) | data formatting | bytes 688128
  48.3 0.0 copy-done.3
  48.3 0.6 %copy.20 = f32[512]{0:T(512)} copy(f32[512]{0:T(512)S(1)} %bitcast.23) | data formatting | bytes 4096
  48.8 0.0 copy-done
  48.8 0.0 copy-start.2
  48.8 0.7 %copy.21 = bf16[512,336]{0,1:T(8,128)(2,1)} copy(bf16[512,336]{0,1:T(8,128)(2,1)S(1)} %bitcast.16) | data formatting | bytes 688128
  49.6 0.0 copy-done.2
  49.6 0.6 %copy.22 = f32[512]{0:T(512)} copy(f32[512]{0:T(512)S(1)} %bitcast.22) | data formatting | bytes 4096
Async XLA Ops:
  45.7 1.8 %copy-start.1 = (bf16[336,512]{1,0:T(8,128)(2,1)S(1)}, bf16[336,512]{1,0:T(8,128)(2,1)}, u32[]{:S(2)}) copy-start(bf16[336,512]{1,0:T(8,128)(2,1)} %get-tuple-element.11) | copy-start | bytes 1032196
  47.5 0.7 %copy-start.3 = (f32[1,512]{1,0:T(1,128)S(1)}, f32[1,512]{1,0:T(1,128)}, u32[]{:S(2)}) copy-start(f32[1,512]{1,0:T(1,128)} %get-tuple-element.12) | copy-start | bytes 6148
  47.5 1.3 %copy-start = (bf16[336,512]{1,0:T(8,128)(2,1)S(1)}, bf16[336,512]{1,0:T(8,128)(2,1)}, u32[]{:S(2)}) copy-start(bf16[336,512]{1,0:T(8,128)(2,1)} %get-tuple-element.13) | copy-start | bytes 1032196
  48.8 0.7 %copy-start.2 = (f32[1,512]{1,0:T(1,128)S(1)}, f32[1,512]{1,0:T(1,128)}, u32[]{:S(2)}) copy-start(f32[1,512]{1,0:T(1,128)} %get-tuple-element.14) | copy-start | bytes 6148

commit v2 on v1

--- a/solution.py
+++ b/solution.py
@@ -1,4 +1,5 @@
 import functools
+import math
 
 import jax
 import jax.numpy as jnp
@@ -19,15 +20,37 @@
 eps_peak = 1e-06
 
 
-def kernel(
+def fold(i, side):
+    half = side // 2
+    return jnp.where(i < half, i, side + half - 1 - i)
+
+
+def dp_rank(d, n):
+    side = math.isqrt(n)
+    return (d % side) * side + fold(d // side, side)
+
+
+def dp_at(r, n):
+    side = math.isqrt(n)
+    return fold(r % side, side) * side + r // side
+
+
+def exchange(
     n_dp, n_mp,
     cot_hbm, tok_hbm, slot_hbm, tab_hbm, mc_hbm, ms_hbm, vc_hbm, vs_hbm,
-    nt_hbm, nm_hbm, nms_hbm, nv_hbm, nvs_hbm,
+    nt, mom, sec, top,
     cot, tok, slot, tab, mc, ms, vc, vs,
-    send, recv, mom, sec, peak, peaks, nt, nm, nv, nms, nvs,
-    in_sems, out_sems, send_sem, recv_sem, psend_sem, precv_sem,
+    send, recv, peak, peaks,
+    in_sems, send_sem, recv_sem, psend_sem, precv_sem, ready, go, mp_in, mp_go,
 ):
     dp, mp = lax.axis_index("dp"), lax.axis_index("mp")
+    side = math.isqrt(n_dp)
+    r_dp = dp_rank(dp, n_dp)
+    level, place_in = r_dp // side, r_dp % side
+    hub = level == 0
+    not_hub = level > 0
+    known = jnp.where(hub, 0, jnp.maximum(level - 2, 1))
+    later = jnp.where(hub, 1, level + 3)
     width, n_tok = cot.shape
     rows = tab.shape[1]
     n_blk = slot.shape[1]
@@ -37,15 +60,6 @@
     strip = 48 if width % 48 == 0 else 16
 
     barrier = pltpu.get_barrier_semaphore()
-
-    def greet_dp(i, _):
-        pl.semaphore_signal(barrier, inc=1, device_id={"dp": lax.rem(dp + i, n_dp)}, device_id_type=MESH)
-        return 0
-
-    def greet_mp(i, _):
-        pl.semaphore_signal(barrier, inc=1, device_id={"mp": lax.rem(mp + i, n_mp)}, device_id_type=MESH)
-        return 0
-
     copies = [
         pltpu.make_async_copy(src, dst, in_sems.at[i])
         for i, (src, dst) in enumerate(
@@ -54,8 +68,34 @@
     ]
     for copy in copies:
         copy.start()
-    lax.fori_loop(1, n_dp, greet_dp, 0)
-    lax.fori_loop(1, n_mp, greet_mp, 0)
+
+    def signal(sem, axis, to):
+        pl.semaphore_signal(sem, inc=1, device_id={axis: to}, device_id_type=MESH)
+
+    def over_levels(low, high, fn):
+        def body(k, _):
+            for i in range(side):
+                fn(k * side + i)
+            return 0
+
+        lax.fori_loop(low, high, body, 0)
+
+    def over_others(fn):
+        for i in range(1, side):
+            fn(level * side + lax.rem(place_in + i, side))
+
+    def over_mp(fn):
+        for i in range(1, n_mp):
+            fn(lax.rem(mp + i, n_mp))
+
+    @pl.when(hub)
+    def _():
+        over_others(lambda r: signal(barrier, "dp", dp_at(r, n_dp)))
+        over_mp(lambda m: signal(barrier, "mp", m))
+
+    over_levels(later, side, lambda r: signal(barrier, "dp", dp_at(r, n_dp)))
+    pl.semaphore_wait(barrier, jnp.where(hub, side + n_mp - 2, known * side))
+    over_levels(0, known, lambda r: signal(ready.at[r_dp], "dp", dp_at(r, n_dp)))
 
     copies[0].wait()
     copies[1].wait()
@@ -84,17 +124,18 @@
     sent = lax.dot_general(chosen, tokens, (((1,), (1,)), ((), ())), preferred_element_type=jnp.float32)
     send[...] = sent.reshape(n_dp, CAP, full).astype(jnp.bfloat16)
 
-    pl.semaphore_wait(barrier, n_dp + n_mp - 2)
-
-    def send_rows(i, _):
-        to = lax.rem(dp + i, n_dp)
-        pltpu.make_async_remote_copy(
+
+    def rows_to(r):
+        to = dp_at(r, n_dp)
+        return pltpu.make_async_remote_copy(
             src_ref=send.at[to], dst_ref=recv.at[dp], send_sem=send_sem, recv_sem=recv_sem,
             device_id={"dp": to}, device_id_type=MESH,
-        ).start()
-        return 0
-
-    lax.fori_loop(1, n_dp, send_rows, 0)
+        )
+
+    def send_to(r):
+        rows_to(r).start()
+
+    over_levels(0, known, send_to)
     recv[pl.ds(dp, 1)] = send[pl.ds(dp, 1)]
 
     for copy in copies[3:]:
@@ -104,6 +145,39 @@
         mom[at, :] = beta_first * (mc[at, :].astype(jnp.float32) * ms[...])
         sec[at, :] = beta_second * (vc[at, :].astype(jnp.float32) * vs[...])
 
+    @pl.when(not_hub)
+    def _():
+        pl.semaphore_wait(go.at[0], 1)
+
+    over_levels(known, jnp.where(hub, 0, level), send_to)
+    over_others(send_to)
+
+    for i in (1, 2):
+
+        @pl.when(jnp.logical_and(not_hub, level + i < side))
+        def _():
+            pl.semaphore_wait(go.at[i], 1)
+            for j in range(side):
+                send_to((level + i) * side + j)
+
+    def next_level(k, _):
+        for i in range(side):
+            pl.semaphore_wait(ready.at[k * side + i], 1)
+            send_to(k * side + i)
+
+        @pl.when(hub)
+        def _():
+            for i in range(3):
+
+                @pl.when(k > i)
+                def _():
+                    signal(go.at[i], "dp", dp_at((k - i) * side + place_in, n_dp))
+
+            over_mp(lambda m: signal(mp_in.at[k], "mp", m))
+
+        return 0
+
+    lax.fori_loop(later, side, next_level, 0)
     others = pl.ds(0, n_dp - 1)
     pltpu.make_async_copy(recv.at[others], recv.at[others], recv_sem).wait()
 
@@ -129,45 +203,58 @@
     peak[0:1, :] = jnp.max(m_top, axis=0, keepdims=True)
     peak[1:2, :] = jnp.max(v_top, axis=0, keepdims=True)
 
-    def send_peak(i, _):
-        to = lax.rem(mp + i, n_mp)
+    @pl.when(not_hub)
+    def _():
+        pl.semaphore_wait(mp_go, 1)
+
+    def send_peak(to):
         pltpu.make_async_remote_copy(
             src_ref=peak, dst_ref=peaks.at[mp], send_sem=psend_sem, recv_sem=precv_sem,
             device_id={"mp": to}, device_id_type=MESH,
         ).start()
-        return 0
-
-    lax.fori_loop(1, n_mp, send_peak, 0)
+
+    over_mp(send_peak)
     peaks[pl.ds(mp, 1)] = peak[...][None]
 
     for c in range(0, width, strip):
         at = pl.ds(c, strip)
         moment, second = mom[at, :], sec[at, :]
         nt[at, :] = (tab[at, :].astype(jnp.float32) - step_rate * (moment / (jnp.sqrt(second) + eps_root))).astype(jnp.bfloat16)
-    outs = [
-        pltpu.make_async_copy(src, dst, out_sems.at[i])
-        for i, (src, dst) in enumerate(((nt, nt_hbm), (nms, nms_hbm), (nvs, nvs_hbm), (nm, nm_hbm), (nv, nv_hbm)))
-    ]
-    outs[0].start()
-
+
+    def mp_level(k, _):
+        pl.semaphore_wait(mp_in.at[k], n_mp - 1)
+        signal(mp_go, "dp", dp_at(k * side + place_in, n_dp))
+        return 0
+
+    lax.fori_loop(1, jnp.where(hub, side, 1), mp_level, 0)
+    pltpu.make_async_copy(send.at[others], send.at[others], send_sem).wait()
     others = pl.ds(0, n_mp - 1)
     pltpu.make_async_copy(peaks.at[others], peaks.at[others], precv_sem).wait()
-    top = jnp.max(peaks[...], axis=0)
+    top[...] = jnp.max(peaks[...], axis=0)
+    pltpu.make_async_copy(peaks.at[others], peaks.at[others], psend_sem).wait()
+
+
+def write(
+    nt, mom, sec, top,
+    nt_hbm, nm_hbm, nms_hbm, nv_hbm, nvs_hbm,
+    nm, nv, nms, nvs, sems,
+):
+    width = nt.shape[0]
+    strip = 112 if width % 112 == 0 else 16
     m_peak, v_peak = top[0:1], top[1:2]
     nms[...] = m_peak
     nvs[...] = v_peak
-    outs[1].start()
-    outs[2].start()
+    outs = [pltpu.make_async_copy(nt, nt_hbm, sems.at[0]), pltpu.make_async_copy(nms, nms_hbm, sems.at[1]), pltpu.make_async_copy(nvs, nvs_hbm, sems.at[2])]
+    for out in outs:
+        out.start()
     m_peak, v_peak = m_peak + eps_peak, v_peak + eps_peak
-    for c in range(0, width, strip):
+    for i, c in enumerate(range(0, width, strip)):
         at = pl.ds(c, strip)
         nm[at, :] = (mom[at, :] / m_peak).astype(jnp.bfloat16)
         nv[at, :] = (sec[at, :] / v_peak).astype(jnp.bfloat16)
-    outs[3].start()
-    outs[4].start()
-    pltpu.make_async_copy(peaks.at[others], peaks.at[others], psend_sem).wait()
-    others = pl.ds(0, n_dp - 1)
-    pltpu.make_async_copy(send.at[others], send.at[others], send_sem).wait()
+        for j, (src, dst) in enumerate(((nm, nm_hbm), (nv, nv_hbm))):
+            outs.append(pltpu.make_async_copy(src.at[at], dst.at[at], sems.at[3 + 2 * i + j]))
+            outs[-1].start()
     for out in outs:
         out.wait()
 
@@ -180,8 +267,48 @@
     full = width // LANES * LANES + LANES
     bf, f32, i32 = jnp.bfloat16, jnp.float32, jnp.int32
     wide, line = (width, rows), (1, rows)
-    outs = pl.pallas_call(
-        functools.partial(kernel, n_dp, n_mp),
+    hbm = pl.BlockSpec(memory_space=pltpu.HBM)
+    vmem = pl.BlockSpec(memory_space=pltpu.VMEM)
+    operands = (
+        cotangent.T, token_ids.reshape(1, -1), block_slot.reshape(1, -1), table.T,
+        m_code.T, m_scale.reshape(line), v_code.T, v_scale.reshape(line),
+    )
+    operands = [pltpu.with_memory_space_constraint(x, pltpu.HBM) for x in operands]
+    held = pl.pallas_call(
+        functools.partial(exchange, n_dp, n_mp),
+        out_shape=(pltpu.VMEM(wide, bf), pltpu.VMEM(wide, f32), pltpu.VMEM(wide, f32), pltpu.VMEM((2, rows), f32)),
+        in_specs=[hbm] * 8,
+        out_specs=[vmem] * 4,
+        scratch_shapes=[
+            pltpu.VMEM((width, n_tok), bf),
+            pltpu.VMEM((1, n_tok), i32),
+            pltpu.VMEM((1, block_slot.shape[0]), i32),
+            pltpu.VMEM(wide, bf),
+            pltpu.VMEM(wide, bf),
+            pltpu.VMEM(line, f32),
+            pltpu.VMEM(wide, bf),
+            pltpu.VMEM(line, f32),
+            pltpu.VMEM((n_dp, CAP, full), bf),
+            pltpu.VMEM((n_dp, CAP, full), bf),
+            pltpu.VMEM((2, rows), f32),
+            pltpu.VMEM((n_mp, 2, rows), f32),
+            pltpu.SemaphoreType.DMA((8,)),
+            pltpu.SemaphoreType.DMA,
+            pltpu.SemaphoreType.DMA,
+            pltpu.SemaphoreType.DMA,
+            pltpu.SemaphoreType.DMA,
+            pltpu.SemaphoreType.REGULAR((n_dp,)),
+            pltpu.SemaphoreType.REGULAR((3,)),
+            pltpu.SemaphoreType.REGULAR((math.isqrt(n_dp),)),
+            pltpu.SemaphoreType.REGULAR,
+        ],
+        compiler_params=pltpu.CompilerParams(
+            collective_id=0, has_side_effects=True, vmem_limit_bytes=32 * 1024 * 1024
+        ),
+        name="embed_adam",
+    )(*operands)
+    new_table, new_m_code, new_m_scale, new_v_code, new_v_scale = pl.pallas_call(
+        write,
         out_shape=(
             jax.ShapeDtypeStruct(wide, bf),
             jax.ShapeDtypeStruct(wide, bf),
@@ -189,44 +316,18 @@
             jax.ShapeDtypeStruct(wide, bf),
             jax.ShapeDtypeStruct(line, f32),
         ),
-        in_specs=[pl.BlockSpec(memory_space=pltpu.HBM)] * 8,
-        out_specs=[pl.BlockSpec(memory_space=pltpu.HBM)] * 5,
+        in_specs=[vmem] * 4,
+        out_specs=[hbm] * 5,
         scratch_shapes=[
-            pltpu.VMEM((width, n_tok), bf),
-            pltpu.VMEM((1, n_tok), i32),
-            pltpu.VMEM((1, block_slot.shape[0]), i32),
-            pltpu.VMEM(wide, bf),
-            pltpu.VMEM(wide, bf),
-            pltpu.VMEM(line, f32),
-            pltpu.VMEM(wide, bf),
-            pltpu.VMEM(line, f32),
-            pltpu.VMEM((n_dp, CAP, full), bf),
-            pltpu.VMEM((n_dp, CAP, full), bf),
-            pltpu.VMEM(wide, f32),
-            pltpu.VMEM(wide, f32),
-            pltpu.VMEM((2, rows), f32),
-            pltpu.VMEM((n_mp, 2, rows), f32),
-            pltpu.VMEM(wide, bf),
             pltpu.VMEM(wide, bf),
             pltpu.VMEM(wide, bf),
             pltpu.VMEM(line, f32),
             pltpu.VMEM(line, f32),
-            pltpu.SemaphoreType.DMA((8,)),
-            pltpu.SemaphoreType.DMA((5,)),
-            pltpu.SemaphoreType.DMA,
-            pltpu.SemaphoreType.DMA,
-            pltpu.SemaphoreType.DMA,
-            pltpu.SemaphoreType.DMA,
+            pltpu.SemaphoreType.DMA((64,)),
         ],
-        compiler_params=pltpu.CompilerParams(
-            collective_id=0, has_side_effects=True, vmem_limit_bytes=63 * 1024 * 1024
-        ),
-        name="embed_adam",
-    )(
-        cotangent.T, token_ids.reshape(1, -1), block_slot.reshape(1, -1), table.T,
-        m_code.T, m_scale.reshape(line), v_code.T, v_scale.reshape(line),
-    )
-    new_table, new_m_code, new_m_scale, new_v_code, new_v_scale = outs
+        compiler_params=pltpu.CompilerParams(vmem_limit_bytes=16 * 1024 * 1024),
+        name="codes",
+    )(*held)
     return (new_table.T, new_m_code.T, new_m_scale.reshape(rows), new_v_code.T, new_v_scale.reshape(rows))
 
 

time: 50.3 us -> 39.3 us (0.78)
  Pallas kernels: 45.1 us -> 38.6 us
  local copies, waits for them, and re-layouts: 4.41 us -> 0 us
    pallas_call x1 -> x2, Pallas kernels: 45.1 us -> 38.6 us  [the longest x1 37 us: per_device(): pl.pallas_call(functools.partial(exchange, n_dp, n_mp), out_shape=(pltpu....]
    unnamed x13 -> x0, local copies, waits for them, and re-layouts: 4.41 us -> none
where the time goes in v2:
time: 39.3 us; the launch traced here: 39.2 us
  Pallas kernels  38.6 us (98%)
  between operations  0.64 us (2%)
    pallas_call x1, Pallas kernels, per_device(): pl.pallas_call(functools.partial(exchange, n_dp, n_mp), out_shape=(pltpu....  37 us
    pallas_call x1, Pallas kernels, per_device(): pl.pallas_call(write, out_shape=(jax.ShapeDtypeStruct(wide, bf), jax.Shap...  1.53 us

profile of v2, /device:TPU:1, one launch (start us, length us, event | category | flops | bytes accessed | tf_op | source)
XLA Modules:
  0.0 39.2 jit_solution(2024381222190282638)
XLA Ops:
  0.6 37.0 %embed_adam.1 = (bf16[336,512]{1,0:T(8,128)(2,1)S(1)}, f32[336,512]{1,0:T(8,128)S(1)}, f32[336,512]{1,0:T(8,128)S(1)}, f32[2,512]{1,0:T(2,128)S(1)}) custom-call(bf16[336,256]{1,0:T(8,128)(2,1)} %bitcast.16, s32[1,256]{1,0:T(1,128)} %bitcast.19, s32[1,128]{1,0:T(1,128)} %bitcast.20, bf16[336,512]{1,0:T(8,128)(2,1)} %bitcast.13, bf16[336,512]{1,0:T(8,128)(2,1)} %bitcast.14, ...), custom_call_target="tpu_custom_call" | custom-call | tf_op jit(solution)/shard_map/embed_adam/pallas_call | solution.py:277
  37.7 1.5 %codes.1 = (bf16[336,512]{1,0:T(8,128)(2,1)}, bf16[336,512]{1,0:T(8,128)(2,1)}, f32[1,512]{1,0:T(1,128)}, bf16[336,512]{1,0:T(8,128)(2,1)}, f32[1,512]{1,0:T(1,128)}) custom-call(bf16[336,512]{1,0:T(8,128)(2,1)S(1)} %get-tuple-element.14.nt, f32[336,512]{1,0:T(8,128)S(1)} %get-tuple-element.15.mom, f32[336,512]{1,0:T(8,128)S(1)} %get-tuple-element.16.sec, ...), custom_call_target="tpu_custom_call" | custom-call | tf_op jit(solution)/shard_map/codes/pallas_call | solution.py:310

commit v3 on v2

--- a/solution.py
+++ b/solution.py
@@ -11,6 +11,7 @@
 BLOCK = 256
 CAP = 8
 LANES = 128
+CUT = 6
 MESH = pl.DeviceIdType.MESH
 
 beta_first = 0.9
@@ -39,9 +40,9 @@
     n_dp, n_mp,
     cot_hbm, tok_hbm, slot_hbm, tab_hbm, mc_hbm, ms_hbm, vc_hbm, vs_hbm,
     nt, mom, sec, top,
-    cot, tok, slot, tab, mc, ms, vc, vs,
-    send, recv, peak, peaks,
-    in_sems, send_sem, recv_sem, psend_sem, precv_sem, ready, go, mp_in, mp_go,
+    cot, tok, slot, scales, codes,
+    send, recv, grad_acc, peak, peaks,
+    in_sems, send_sem, recv_sems, psend_sem, precv_sem, ready, go, mp_in, mp_go,
 ):
     dp, mp = lax.axis_index("dp"), lax.axis_index("mp")
     side = math.isqrt(n_dp)
@@ -49,10 +50,14 @@
     level, place_in = r_dp // side, r_dp % side
     hub = level == 0
     not_hub = level > 0
+    n_early = side * CUT // 8 * side
+    late = (r_dp >= n_early).astype(jnp.int32)
     known = jnp.where(hub, 0, jnp.maximum(level - 2, 1))
     later = jnp.where(hub, 1, level + 3)
     width, n_tok = cot.shape
-    rows = tab.shape[1]
+    rows = codes.shape[2]
+    ms, vs = scales.at[0], scales.at[1]
+    mc, vc, tab = codes.at[0], codes.at[1], codes.at[2]
     n_blk = slot.shape[1]
     n_slot = n_dp * CAP
     full = send.shape[2]
@@ -62,8 +67,9 @@
     barrier = pltpu.get_barrier_semaphore()
     copies = [
         pltpu.make_async_copy(src, dst, in_sems.at[i])
-        for i, (src, dst) in enumerate(
-            ((tok_hbm, tok), (slot_hbm, slot), (cot_hbm, cot), (ms_hbm, ms), (vs_hbm, vs), (mc_hbm, mc), (vc_hbm, vc), (tab_hbm, tab))
+        for i, src, dst in (
+            (0, tok_hbm, tok), (1, slot_hbm, slot), (2, cot_hbm, cot),
+            (3, ms_hbm, ms), (3, vs_hbm, vs), (4, mc_hbm, mc), (4, vc_hbm, vc), (4, tab_hbm, tab),
         )
     ]
     for copy in copies:
@@ -93,10 +99,15 @@
         over_others(lambda r: signal(barrier, "dp", dp_at(r, n_dp)))
         over_mp(lambda m: signal(barrier, "mp", m))
 
+    @pl.when(not_hub)
+    def _():
+        signal(barrier, "mp", mp + 1 - 2 * lax.rem(mp, 2))
+
     over_levels(later, side, lambda r: signal(barrier, "dp", dp_at(r, n_dp)))
-    pl.semaphore_wait(barrier, jnp.where(hub, side + n_mp - 2, known * side))
-    over_levels(0, known, lambda r: signal(ready.at[r_dp], "dp", dp_at(r, n_dp)))
-
+    pl.semaphore_wait(barrier, jnp.where(hub, side + n_mp - 2, known * side + 1))
+    earlier = (
+        lax.broadcasted_iota(jnp.int32, (n_tok, n_tok), 0) < lax.broadcasted_iota(jnp.int32, (n_tok, n_tok), 1)
+    ).astype(jnp.bfloat16)
     copies[0].wait()
     copies[1].wait()
     ids = tok[...]
@@ -108,9 +119,6 @@
     owner = held // 2
     sub = held % 2
     of_owner = (lax.broadcasted_iota(jnp.int32, (n_dp, n_tok), 0) == owner).astype(jnp.float32)
-    earlier = (
-        lax.broadcasted_iota(jnp.int32, (n_tok, n_tok), 0) < lax.broadcasted_iota(jnp.int32, (n_tok, n_tok), 1)
-    ).astype(jnp.bfloat16)
     before = jnp.dot(of_owner.astype(jnp.bfloat16), earlier, preferred_element_type=jnp.float32)
     rank = jnp.sum(of_owner * before, axis=0, keepdims=True)
     place = owner * CAP + rank.astype(jnp.int32)
@@ -128,23 +136,25 @@
     def rows_to(r):
         to = dp_at(r, n_dp)
         return pltpu.make_async_remote_copy(
-            src_ref=send.at[to], dst_ref=recv.at[dp], send_sem=send_sem, recv_sem=recv_sem,
+            src_ref=send.at[to], dst_ref=recv.at[r_dp], send_sem=send_sem, recv_sem=recv_sems.at[late],
             device_id={"dp": to}, device_id_type=MESH,
         )
 
     def send_to(r):
         rows_to(r).start()
 
-    over_levels(0, known, send_to)
-    recv[pl.ds(dp, 1)] = send[pl.ds(dp, 1)]
-
-    for copy in copies[3:]:
-        copy.wait()
+    over_levels(0, jnp.minimum(known, 1), send_to)
+    over_levels(0, known, lambda r: signal(ready.at[level], "dp", dp_at(r, n_dp)))
+    recv[pl.ds(r_dp, 1)] = send[pl.ds(dp, 1)]
+
+    pltpu.make_async_copy(scales, scales, in_sems.at[3]).wait()
+    pltpu.make_async_copy(codes, codes, in_sems.at[4]).wait()
     for c in range(0, width, strip):
         at = pl.ds(c, strip)
         mom[at, :] = beta_first * (mc[at, :].astype(jnp.float32) * ms[...])
         sec[at, :] = beta_second * (vc[at, :].astype(jnp.float32) * vs[...])
 
+    over_levels(1, known, send_to)
     @pl.when(not_hub)
     def _():
         pl.semaphore_wait(go.at[0], 1)
@@ -161,8 +171,8 @@
                 send_to((level + i) * side + j)
 
     def next_level(k, _):
+        pl.semaphore_wait(ready.at[k], side)
         for i in range(side):
-            pl.semaphore_wait(ready.at[k * side + i], 1)
             send_to(k * side + i)
 
         @pl.when(hub)
@@ -173,27 +183,41 @@
                 def _():
                     signal(go.at[i], "dp", dp_at((k - i) * side + place_in, n_dp))
 
-            over_mp(lambda m: signal(mp_in.at[k], "mp", m))
+            over_mp(lambda m: signal(mp_in, "mp", m))
 
         return 0
 
     lax.fori_loop(later, side, next_level, 0)
     others = pl.ds(0, n_dp - 1)
-    pltpu.make_async_copy(recv.at[others], recv.at[others], recv_sem).wait()
-
-    got = recv[...].astype(jnp.float32).reshape(n_slot, full).astype(jnp.bfloat16)
     last = full - LANES
     pick = (lax.broadcasted_iota(jnp.int32, (LANES, rows), 0) >= width - last).astype(jnp.bfloat16)
-    index = jnp.dot(got[:, last:full], pick, preferred_element_type=jnp.float32).astype(jnp.int32)
-    row = lax.broadcasted_iota(jnp.int32, (n_slot, rows), 1) + BLOCK
-    selector = (row == index).astype(jnp.bfloat16)
-    grad = lax.dot_general(got, selector, (((0,), (0,)), ((), ())), preferred_element_type=jnp.float32)
+
+    def wait_rows(part, n):
+        @pl.when(late == part)
+        def _():
+            pltpu.make_async_copy(recv.at[pl.ds(0, n - 1)], recv.at[pl.ds(0, n - 1)], recv_sems.at[part]).wait()
+
+        @pl.when(late != part)
+        def _():
+            pltpu.make_async_copy(recv.at[pl.ds(0, n)], recv.at[pl.ds(0, n)], recv_sems.at[part]).wait()
+
+    def sum_rows(first, n):
+        got = recv[first : first + n].astype(jnp.float32).reshape(n * CAP, full).astype(jnp.bfloat16)
+        index = jnp.dot(got[:, last:full], pick, preferred_element_type=jnp.float32).astype(jnp.int32)
+        row = lax.broadcasted_iota(jnp.int32, (n * CAP, rows), 1) + BLOCK
+        selector = (row == index).astype(jnp.bfloat16)
+        return lax.dot_general(got, selector, (((0,), (0,)), ((), ())), preferred_element_type=jnp.float32)
+
+    wait_rows(0, n_early)
+    grad_acc[...] = sum_rows(0, n_early)
+    wait_rows(1, n_dp - n_early)
+    grad = sum_rows(n_early, n_dp - n_early)
 
     m_top = jnp.zeros((8, rows), jnp.float32)
     v_top = jnp.zeros((8, rows), jnp.float32)
     for c in range(0, width, strip):
         at = pl.ds(c, strip)
-        g = grad[c : c + strip]
+        g = grad_acc[at, :] + grad[c : c + strip]
         moment = mom[at, :] + 0.1 * g
         second = sec[at, :] + 0.05 * (g * g)
         mom[at, :] = moment
@@ -213,7 +237,11 @@
             device_id={"mp": to}, device_id_type=MESH,
         ).start()
 
-    over_mp(send_peak)
+    chips = n_mp // 2
+    for i in sorted(range(chips), key=lambda i: -min(i, chips - i)):
+        for core in (0, 1):
+            if i or core:
+                send_peak(lax.rem(mp // 2 + i, chips) * 2 + lax.rem(mp + core, 2))
     peaks[pl.ds(mp, 1)] = peak[...][None]
 
     for c in range(0, width, strip):
@@ -221,17 +249,22 @@
         moment, second = mom[at, :], sec[at, :]
         nt[at, :] = (tab[at, :].astype(jnp.float32) - step_rate * (moment / (jnp.sqrt(second) + eps_root))).astype(jnp.bfloat16)
 
-    def mp_level(k, _):
-        pl.semaphore_wait(mp_in.at[k], n_mp - 1)
-        signal(mp_go, "dp", dp_at(k * side + place_in, n_dp))
-        return 0
-
-    lax.fori_loop(1, jnp.where(hub, side, 1), mp_level, 0)
+    @pl.when(hub)
+    def _():
+        pl.semaphore_wait(mp_in, (n_mp - 1) * (side - 1))
+        for k in range(1, side):
+            signal(mp_go, "dp", dp_at(k * side + place_in, n_dp))
+
     pltpu.make_async_copy(send.at[others], send.at[others], send_sem).wait()
     others = pl.ds(0, n_mp - 1)
     pltpu.make_async_copy(peaks.at[others], peaks.at[others], precv_sem).wait()
     top[...] = jnp.max(peaks[...], axis=0)
     pltpu.make_async_copy(peaks.at[others], peaks.at[others], psend_sem).wait()
+
+
+def strips(width):
+    strip = 112 if width % 112 == 0 else 16
+    return [pl.ds(c, strip) for c in range(0, width, strip)]
 
 
 def write(
@@ -240,7 +273,6 @@
     nm, nv, nms, nvs, sems,
 ):
     width = nt.shape[0]
-    strip = 112 if width % 112 == 0 else 16
     m_peak, v_peak = top[0:1], top[1:2]
     nms[...] = m_peak
     nvs[...] = v_peak
@@ -248,8 +280,7 @@
     for out in outs:
         out.start()
     m_peak, v_peak = m_peak + eps_peak, v_peak + eps_peak
-    for i, c in enumerate(range(0, width, strip)):
-        at = pl.ds(c, strip)
+    for i, at in enumerate(strips(width)):
         nm[at, :] = (mom[at, :] / m_peak).astype(jnp.bfloat16)
         nv[at, :] = (sec[at, :] / v_peak).astype(jnp.bfloat16)
         for j, (src, dst) in enumerate(((nm, nm_hbm), (nv, nv_hbm))):
@@ -267,6 +298,7 @@
     full = width // LANES * LANES + LANES
     bf, f32, i32 = jnp.bfloat16, jnp.float32, jnp.int32
     wide, line = (width, rows), (1, rows)
+    side = math.isqrt(n_dp)
     hbm = pl.BlockSpec(memory_space=pltpu.HBM)
     vmem = pl.BlockSpec(memory_space=pltpu.VMEM)
     operands = (
@@ -283,23 +315,21 @@
             pltpu.VMEM((width, n_tok), bf),
             pltpu.VMEM((1, n_tok), i32),
             pltpu.VMEM((1, block_slot.shape[0]), i32),
-            pltpu.VMEM(wide, bf),
-            pltpu.VMEM(wide, bf),
-            pltpu.VMEM(line, f32),
-            pltpu.VMEM(wide, bf),
-            pltpu.VMEM(line, f32),
+            pltpu.VMEM((2, 1, rows), f32),
+            pltpu.VMEM((3, *wide), bf),
             pltpu.VMEM((n_dp, CAP, full), bf),
             pltpu.VMEM((n_dp, CAP, full), bf),
+            pltpu.VMEM((full, rows), f32),
             pltpu.VMEM((2, rows), f32),
             pltpu.VMEM((n_mp, 2, rows), f32),
-            pltpu.SemaphoreType.DMA((8,)),
+            pltpu.SemaphoreType.DMA((5,)),
+            pltpu.SemaphoreType.DMA,
+            pltpu.SemaphoreType.DMA((2,)),
             pltpu.SemaphoreType.DMA,
             pltpu.SemaphoreType.DMA,
-            pltpu.SemaphoreType.DMA,
-            pltpu.SemaphoreType.DMA,
-            pltpu.SemaphoreType.REGULAR((n_dp,)),
+            pltpu.SemaphoreType.REGULAR((side,)),
             pltpu.SemaphoreType.REGULAR((3,)),
-            pltpu.SemaphoreType.REGULAR((math.isqrt(n_dp),)),
+            pltpu.SemaphoreType.REGULAR,
             pltpu.SemaphoreType.REGULAR,
         ],
         compiler_params=pltpu.CompilerParams(
@@ -323,7 +353,7 @@
             pltpu.VMEM(wide, bf),
             pltpu.VMEM(line, f32),
             pltpu.VMEM(line, f32),
-            pltpu.SemaphoreType.DMA((64,)),
+            pltpu.SemaphoreType.DMA((3 + 2 * len(strips(width)),)),
         ],
         compiler_params=pltpu.CompilerParams(vmem_limit_bytes=16 * 1024 * 1024),
         name="codes",

time: 39.3 us -> 37.5 us (0.954)
  Pallas kernels: 38.6 us -> 36.8 us
    pallas_call x1, Pallas kernels: 37 us -> 35.7 us  [per_device(): pl.pallas_call(functools.partial(exchange, n_dp, n_mp), out_shape=(pltpu....]
    pallas_call x1, Pallas kernels: 1.53 us -> 1.04 us  [per_device(): pl.pallas_call(write, out_shape=(jax.ShapeDtypeStruct(wide, bf), jax.Shap...]
where the time goes in v3:
time: 37.5 us; the launch traced here: 37.4 us
  Pallas kernels  36.8 us (98%)
  between operations  0.64 us (2%)
    pallas_call x1, Pallas kernels, per_device(): pl.pallas_call(functools.partial(exchange, n_dp, n_mp), out_shape=(pltpu....  35.7 us
    pallas_call x1, Pallas kernels, per_device(): pl.pallas_call(write, out_shape=(jax.ShapeDtypeStruct(wide, bf), jax.Shap...  1.04 us

profile of v3, /device:TPU:1, one launch (start us, length us, event | category | flops | bytes accessed | tf_op | source)
XLA Modules:
  0.0 37.4 jit_solution(3612624685137310281)
XLA Ops:
  0.6 35.7 %embed_adam.1 = (bf16[336,512]{1,0:T(8,128)(2,1)S(1)}, f32[336,512]{1,0:T(8,128)S(1)}, f32[336,512]{1,0:T(8,128)S(1)}, f32[2,512]{1,0:T(2,128)S(1)}) custom-call(bf16[336,256]{1,0:T(8,128)(2,1)} %bitcast.16, s32[1,256]{1,0:T(1,128)} %bitcast.19, s32[1,128]{1,0:T(1,128)} %bitcast.20, bf16[336,512]{1,0:T(8,128)(2,1)} %bitcast.13, bf16[336,512]{1,0:T(8,128)(2,1)} %bitcast.14, ...), custom_call_target="tpu_custom_call" | custom-call | tf_op jit(solution)/shard_map/embed_adam/pallas_call | solution.py:309
  36.4 1.0 %codes.1 = (bf16[336,512]{1,0:T(8,128)(2,1)}, bf16[336,512]{1,0:T(8,128)(2,1)}, f32[1,512]{1,0:T(1,128)}, bf16[336,512]{1,0:T(8,128)(2,1)}, f32[1,512]{1,0:T(1,128)}) custom-call(bf16[336,512]{1,0:T(8,128)(2,1)S(1)} %get-tuple-element.14.nt, f32[336,512]{1,0:T(8,128)S(1)} %get-tuple-element.15.mom, f32[336,512]{1,0:T(8,128)S(1)} %get-tuple-element.16.sec, ...), custom_call_target="tpu_custom_call" | custom-call | tf_op jit(solution)/shard_map/codes/pallas_call | solution.py:340

commit v4 on v3

--- a/solution.py
+++ b/solution.py
@@ -11,7 +11,7 @@
 BLOCK = 256
 CAP = 8
 LANES = 128
-CUT = 6
+CUT = 7
 MESH = pl.DeviceIdType.MESH
 
 beta_first = 0.9
@@ -34,6 +34,18 @@
 def dp_at(r, n):
     side = math.isqrt(n)
     return fold(r % side, side) * side + r // side
+
+
+LATER = {8: (1, 4, 5, 8, 8, 8, 8, 8), 4: (1, 3, 4, 4), 2: (1, 2)}
+SPREAD = max(later - level for table in LATER.values() for level, later in enumerate(table) if level)
+
+
+def later_than(level, side):
+    return sum(jnp.where(level == j, later, 0) for j, later in enumerate(LATER[side]))
+
+
+def known_to(level, side):
+    return sum(jnp.where(level >= later, 1, 0) for later in LATER[side])
 
 
 def exchange(
@@ -42,18 +54,19 @@
     nt, mom, sec, top,
     cot, tok, slot, scales, codes,
     send, recv, grad_acc, peak, peaks,
-    in_sems, send_sem, recv_sems, psend_sem, precv_sem, ready, go, mp_in, mp_go,
+    in_sems, send_sem, recv_sems, psend_sem, precv_sem, ready, mine, below, go, mp_in, mp_go, pal,
 ):
     dp, mp = lax.axis_index("dp"), lax.axis_index("mp")
     side = math.isqrt(n_dp)
     r_dp = dp_rank(dp, n_dp)
     level, place_in = r_dp // side, r_dp % side
     hub = level == 0
+    middle = side // 2
     not_hub = level > 0
     n_early = side * CUT // 8 * side
     late = (r_dp >= n_early).astype(jnp.int32)
-    known = jnp.where(hub, 0, jnp.maximum(level - 2, 1))
-    later = jnp.where(hub, 1, level + 3)
+    known = known_to(level, side)
+    later = later_than(level, side)
     width, n_tok = cot.shape
     rows = codes.shape[2]
     ms, vs = scales.at[0], scales.at[1]
@@ -65,6 +78,7 @@
     strip = 48 if width % 48 == 0 else 16
 
     barrier = pltpu.get_barrier_semaphore()
+    partner = mp + 1 - 2 * lax.rem(mp, 2)
     copies = [
         pltpu.make_async_copy(src, dst, in_sems.at[i])
         for i, src, dst in (
@@ -101,10 +115,16 @@
 
     @pl.when(not_hub)
     def _():
-        signal(barrier, "mp", mp + 1 - 2 * lax.rem(mp, 2))
+        signal(barrier, "mp", partner)
 
     over_levels(later, side, lambda r: signal(barrier, "dp", dp_at(r, n_dp)))
     pl.semaphore_wait(barrier, jnp.where(hub, side + n_mp - 2, known * side + 1))
+    @pl.when(not_hub)
+    def _():
+        signal(mine.at[level], "dp", dp_at(place_in, n_dp))
+
+    over_levels(0, known, lambda r: signal(ready.at[level], "dp", dp_at(r, n_dp)))
+
     earlier = (
         lax.broadcasted_iota(jnp.int32, (n_tok, n_tok), 0) < lax.broadcasted_iota(jnp.int32, (n_tok, n_tok), 1)
     ).astype(jnp.bfloat16)
@@ -121,22 +141,26 @@
     of_owner = (lax.broadcasted_iota(jnp.int32, (n_dp, n_tok), 0) == owner).astype(jnp.float32)
     before = jnp.dot(of_owner.astype(jnp.bfloat16), earlier, preferred_element_type=jnp.float32)
     rank = jnp.sum(of_owner * before, axis=0, keepdims=True)
-    place = owner * CAP + rank.astype(jnp.int32)
-    chosen = (lax.broadcasted_iota(jnp.int32, (n_slot, n_tok), 0) == place).astype(jnp.bfloat16)
+    place = dp_rank(owner, n_dp) * CAP + rank.astype(jnp.int32)
 
     meta_row = lax.broadcasted_iota(jnp.int32, (n_meta, n_tok), 0)
     meta = jnp.where(meta_row == 0, low, jnp.where(meta_row == 1, (sub + 1) * BLOCK, 0))
     meta = meta.astype(jnp.float32).astype(jnp.bfloat16)
     copies[2].wait()
     tokens = jnp.concatenate([cot[...], meta], axis=0)
-    sent = lax.dot_general(chosen, tokens, (((1,), (1,)), ((), ())), preferred_element_type=jnp.float32)
-    send[...] = sent.reshape(n_dp, CAP, full).astype(jnp.bfloat16)
-
+
+    def fill(first, n):
+        slots = lax.broadcasted_iota(jnp.int32, (n * CAP, n_tok), 0) + first * CAP
+        chosen = (slots == place).astype(jnp.bfloat16)
+        rows_sent = lax.dot_general(chosen, tokens, (((1,), (1,)), ((), ())), preferred_element_type=jnp.float32)
+        send[first : first + n] = rows_sent.reshape(n, CAP, full).astype(jnp.bfloat16)
+
+    fill(0, side)
 
     def rows_to(r):
         to = dp_at(r, n_dp)
         return pltpu.make_async_remote_copy(
-            src_ref=send.at[to], dst_ref=recv.at[r_dp], send_sem=send_sem, recv_sem=recv_sems.at[late],
+            src_ref=send.at[r], dst_ref=recv.at[r_dp], send_sem=send_sem, recv_sem=recv_sems.at[late],
             device_id={"dp": to}, device_id_type=MESH,
         )
 
@@ -144,8 +168,13 @@
         rows_to(r).start()
 
     over_levels(0, jnp.minimum(known, 1), send_to)
-    over_levels(0, known, lambda r: signal(ready.at[level], "dp", dp_at(r, n_dp)))
-    recv[pl.ds(r_dp, 1)] = send[pl.ds(dp, 1)]
+
+    @pl.when(known > 1)
+    def _():
+        signal(pal, "mp", partner)
+
+    fill(side, n_dp - side)
+    recv[pl.ds(r_dp, 1)] = send[pl.ds(r_dp, 1)]
 
     pltpu.make_async_copy(scales, scales, in_sems.at[3]).wait()
     pltpu.make_async_copy(codes, codes, in_sems.at[4]).wait()
@@ -154,32 +183,62 @@
         mom[at, :] = beta_first * (mc[at, :].astype(jnp.float32) * ms[...])
         sec[at, :] = beta_second * (vc[at, :].astype(jnp.float32) * vs[...])
 
-    over_levels(1, known, send_to)
+    def known_level(k, _):
+        pl.semaphore_wait(pal, 1)
+        for i in range(side):
+            send_to(k * side + i)
+
+        @pl.when(k + 1 < known)
+        def _():
+            signal(pal, "mp", partner)
+
+        return 0
+
+    lax.fori_loop(1, known, known_level, 0)
+
     @pl.when(not_hub)
     def _():
+        pl.semaphore_wait(below, 1)
+
+    over_levels(known, jnp.where(hub, 0, jnp.minimum(level, middle)), send_to)
+    @pl.when(not_hub)
+    def _():
         pl.semaphore_wait(go.at[0], 1)
 
-    over_levels(known, jnp.where(hub, 0, level), send_to)
+    over_levels(middle, level, send_to)
     over_others(send_to)
 
-    for i in (1, 2):
-
-        @pl.when(jnp.logical_and(not_hub, level + i < side))
+    for i in range(1, SPREAD):
+
+        @pl.when(jnp.logical_and(not_hub, level + i < later))
         def _():
             pl.semaphore_wait(go.at[i], 1)
             for j in range(side):
                 send_to((level + i) * side + j)
 
+    def tell_below(k):
+        pl.semaphore_wait(mine.at[k], 1)
+        signal(below, "dp", dp_at(k * side + place_in, n_dp))
+
     def next_level(k, _):
+        @pl.when(jnp.logical_and(hub, k <= middle))
+        def _():
+            tell_below(k)
+
+        @pl.when(jnp.logical_and(hub, k == middle))
+        def _():
+            for j in range(middle + 1, side):
+                tell_below(j)
+
         pl.semaphore_wait(ready.at[k], side)
         for i in range(side):
             send_to(k * side + i)
 
         @pl.when(hub)
         def _():
-            for i in range(3):
-
-                @pl.when(k > i)
+            for i in range(SPREAD):
+
+                @pl.when(jnp.logical_and(k > i, k < later_than(k - i, side)))
                 def _():
                     signal(go.at[i], "dp", dp_at((k - i) * side + place_in, n_dp))
 
@@ -263,7 +322,7 @@
 
 
 def strips(width):
-    strip = 112 if width % 112 == 0 else 16
+    strip = 48 if width % 48 == 0 else 16
     return [pl.ds(c, strip) for c in range(0, width, strip)]
 
 
@@ -276,18 +335,26 @@
     m_peak, v_peak = top[0:1], top[1:2]
     nms[...] = m_peak
     nvs[...] = v_peak
-    outs = [pltpu.make_async_copy(nt, nt_hbm, sems.at[0]), pltpu.make_async_copy(nms, nms_hbm, sems.at[1]), pltpu.make_async_copy(nvs, nvs_hbm, sems.at[2])]
-    for out in outs:
-        out.start()
+    parts = strips(width)
+
+    def put(src, dst, sem, at):
+        pltpu.make_async_copy(src.at[at], dst.at[at], sems.at[sem]).start()
+
+    for at in parts:
+        put(nt, nt_hbm, 0, at)
+    lines = [pltpu.make_async_copy(nms, nms_hbm, sems.at[3]), pltpu.make_async_copy(nvs, nvs_hbm, sems.at[4])]
+    for line in lines:
+        line.start()
     m_peak, v_peak = m_peak + eps_peak, v_peak + eps_peak
-    for i, at in enumerate(strips(width)):
+    for at in parts:
         nm[at, :] = (mom[at, :] / m_peak).astype(jnp.bfloat16)
+        put(nm, nm_hbm, 1, at)
         nv[at, :] = (sec[at, :] / v_peak).astype(jnp.bfloat16)
-        for j, (src, dst) in enumerate(((nm, nm_hbm), (nv, nv_hbm))):
-            outs.append(pltpu.make_async_copy(src.at[at], dst.at[at], sems.at[3 + 2 * i + j]))
-            outs[-1].start()
-    for out in outs:
-        out.wait()
+        put(nv, nv_hbm, 2, at)
+    for i, (src, dst) in enumerate(((nt, nt_hbm), (nm, nm_hbm), (nv, nv_hbm))):
+        pltpu.make_async_copy(src, dst, sems.at[i]).wait()
+    for line in lines:
+        line.wait()
 
 
 def per_device(cotangent, token_ids, block_counts, block_slot, table, m_code, m_scale, v_code, v_scale):
@@ -328,7 +395,10 @@
             pltpu.SemaphoreType.DMA,
             pltpu.SemaphoreType.DMA,
             pltpu.SemaphoreType.REGULAR((side,)),
-            pltpu.SemaphoreType.REGULAR((3,)),
+            pltpu.SemaphoreType.REGULAR((side,)),
+            pltpu.SemaphoreType.REGULAR,
+            pltpu.SemaphoreType.REGULAR((SPREAD,)),
+            pltpu.SemaphoreType.REGULAR,
             pltpu.SemaphoreType.REGULAR,
             pltpu.SemaphoreType.REGULAR,
         ],
@@ -353,7 +423,7 @@
             pltpu.VMEM(wide, bf),
             pltpu.VMEM(line, f32),
             pltpu.VMEM(line, f32),
-            pltpu.SemaphoreType.DMA((3 + 2 * len(strips(width)),)),
+            pltpu.SemaphoreType.DMA((5,)),
         ],
         compiler_params=pltpu.CompilerParams(vmem_limit_bytes=16 * 1024 * 1024),
         name="codes",

time: 37.5 us -> 36.2 us (0.965)
  Pallas kernels: 36.8 us -> 35.4 us
    pallas_call x1, Pallas kernels: 35.7 us -> 34.4 us  [per_device(): pl.pallas_call(functools.partial(exchange, n_dp, n_mp), out_shape=(pltpu....]
where the time goes in v4:
time: 36.2 us; the launch traced here: 36.1 us
  Pallas kernels  35.4 us (98%)
  between operations  0.64 us (2%)
    pallas_call x1, Pallas kernels, per_device(): pl.pallas_call(functools.partial(exchange, n_dp, n_mp), out_shape=(pltpu....  34.4 us
    pallas_call x1, Pallas kernels, per_device(): pl.pallas_call(write, out_shape=(jax.ShapeDtypeStruct(wide, bf), jax.Shap...  1 us

profile of v4, /device:TPU:1, one launch (start us, length us, event | category | flops | bytes accessed | tf_op | source)
XLA Modules:
  0.0 36.1 jit_solution(17369328024409939699)
XLA Ops:
  0.6 34.4 %embed_adam.1 = (bf16[336,512]{1,0:T(8,128)(2,1)S(1)}, f32[336,512]{1,0:T(8,128)S(1)}, f32[336,512]{1,0:T(8,128)S(1)}, f32[2,512]{1,0:T(2,128)S(1)}) custom-call(bf16[336,256]{1,0:T(8,128)(2,1)} %bitcast.16, s32[1,256]{1,0:T(1,128)} %bitcast.19, s32[1,128]{1,0:T(1,128)} %bitcast.20, bf16[336,512]{1,0:T(8,128)(2,1)} %bitcast.13, bf16[336,512]{1,0:T(8,128)(2,1)} %bitcast.14, ...), custom_call_target="tpu_custom_call" | custom-call | tf_op jit(solution)/shard_map/embed_adam/pallas_call | solution.py:376
  35.1 1.0 %codes.1 = (bf16[336,512]{1,0:T(8,128)(2,1)}, bf16[336,512]{1,0:T(8,128)(2,1)}, f32[1,512]{1,0:T(1,128)}, bf16[336,512]{1,0:T(8,128)(2,1)}, f32[1,512]{1,0:T(1,128)}) custom-call(bf16[336,512]{1,0:T(8,128)(2,1)S(1)} %get-tuple-element.14.nt, f32[336,512]{1,0:T(8,128)S(1)} %get-tuple-element.15.mom, f32[336,512]{1,0:T(8,128)S(1)} %get-tuple-element.16.sec, ...), custom_call_target="tpu_custom_call" | custom-call | tf_op jit(solution)/shard_map/codes/pallas_call | solution.py:410

commit v5 on v4

--- a/solution.py
+++ b/solution.py
@@ -108,16 +108,22 @@
         for i in range(1, n_mp):
             fn(lax.rem(mp + i, n_mp))
 
+    def greet_level(i, _):
+        for j in range(side):
+            signal(barrier, "dp", dp_at((side - 1 - i) * side + j, n_dp))
+        return 0
+
+    lax.fori_loop(0, side - later, greet_level, 0)
+
+    @pl.when(not_hub)
+    def _():
+        signal(barrier, "mp", partner)
+
     @pl.when(hub)
     def _():
         over_others(lambda r: signal(barrier, "dp", dp_at(r, n_dp)))
         over_mp(lambda m: signal(barrier, "mp", m))
 
-    @pl.when(not_hub)
-    def _():
-        signal(barrier, "mp", partner)
-
-    over_levels(later, side, lambda r: signal(barrier, "dp", dp_at(r, n_dp)))
     pl.semaphore_wait(barrier, jnp.where(hub, side + n_mp - 2, known * side + 1))
     @pl.when(not_hub)
     def _():
@@ -183,6 +189,12 @@
         mom[at, :] = beta_first * (mc[at, :].astype(jnp.float32) * ms[...])
         sec[at, :] = beta_second * (vc[at, :].astype(jnp.float32) * vs[...])
 
+    last_level = level == side - 1
+
+    @pl.when(last_level)
+    def _():
+        pl.semaphore_wait(below, 1)
+
     def known_level(k, _):
         pl.semaphore_wait(pal, 1)
         for i in range(side):
@@ -196,7 +208,7 @@
 
     lax.fori_loop(1, known, known_level, 0)
 
-    @pl.when(not_hub)
+    @pl.when(jnp.logical_and(not_hub, jnp.logical_not(last_level)))
     def _():
         pl.semaphore_wait(below, 1)
 

time: 36.2 us -> 35.8 us (0.989)
  Pallas kernels: 35.4 us -> 35 us
    pallas_call x1, Pallas kernels: 34.4 us -> 34 us  [per_device(): pl.pallas_call(functools.partial(exchange, n_dp, n_mp), out_shape=(pltpu....]
where the time goes in v5:
time: 35.8 us; the launch traced here: 35.7 us
  Pallas kernels  35 us (98%)
  between operations  0.64 us (2%)
    pallas_call x1, Pallas kernels, per_device(): pl.pallas_call(functools.partial(exchange, n_dp, n_mp), out_shape=(pltpu....  34 us
    pallas_call x1, Pallas kernels, per_device(): pl.pallas_call(write, out_shape=(jax.ShapeDtypeStruct(wide, bf), jax.Shap...  1 us

profile of v5, /device:TPU:1, one launch (start us, length us, event | category | flops | bytes accessed | tf_op | source)
XLA Modules:
  0.0 35.7 jit_solution(16726733849704726297)
XLA Ops:
  0.6 34.0 %embed_adam.1 = (bf16[336,512]{1,0:T(8,128)(2,1)S(1)}, f32[336,512]{1,0:T(8,128)S(1)}, f32[336,512]{1,0:T(8,128)S(1)}, f32[2,512]{1,0:T(2,128)S(1)}) custom-call(bf16[336,256]{1,0:T(8,128)(2,1)} %bitcast.16, s32[1,256]{1,0:T(1,128)} %bitcast.19, s32[1,128]{1,0:T(1,128)} %bitcast.20, bf16[336,512]{1,0:T(8,128)(2,1)} %bitcast.13, bf16[336,512]{1,0:T(8,128)(2,1)} %bitcast.14, ...), custom_call_target="tpu_custom_call" | custom-call | tf_op jit(solution)/shard_map/embed_adam/pallas_call | solution.py:388
  34.7 1.0 %codes.1 = (bf16[336,512]{1,0:T(8,128)(2,1)}, bf16[336,512]{1,0:T(8,128)(2,1)}, f32[1,512]{1,0:T(1,128)}, bf16[336,512]{1,0:T(8,128)(2,1)}, f32[1,512]{1,0:T(1,128)}) custom-call(bf16[336,512]{1,0:T(8,128)(2,1)S(1)} %get-tuple-element.14.nt, f32[336,512]{1,0:T(8,128)S(1)} %get-tuple-element.15.mom, f32[336,512]{1,0:T(8,128)S(1)} %get-tuple-element.16.sec, ...), custom_call_target="tpu_custom_call" | custom-call | tf_op jit(solution)/shard_map/codes/pallas_call | solution.py:422
